TPU v7x, 32 devices: a whole 2x2x4 slice. The times are simulated.
32 devices in a mesh: row: 8 (over y, x, core), col: 4 (over z).
Axes of the slice: x: 2, y: 2, z: 4, core: 2. Of those that a mesh axis runs over, the one named last changes fastest.
Arguments:
- item_factors: bfloat16 [4096, 128], P(('row', 'col')), may hold values from -0.5 to 0.5
- item_index: int32 [256, 2048], P('col', 'row'), may hold values from 0 to 511
- ratings: bfloat16 [256, 2048], P('col', 'row'), may hold values from -4 to 4
- counts: int32 [256, 8], P('col', 'row'), may hold values from 1 to 256, as said below
Outputs:
- user_factors: float32 [4, 64, 128], P('col', 'row')
Inputs may be any that keep to these rules, and one draw needn't show every extreme that they name: `counts`: for each user block and item block, some user has exactly 256 live slots.
All inputs are finite; a program needn't handle non-finite values.
Results may differ from a plain program's by a relative error of at most 0.0004.
Values may be sent and summed in bfloat16 or wider, within the bound.
A program may use at most 192 MiB of HBM per device.

v0:
```python
import jax
import jax.numpy as jnp
from jax import lax
from jax.sharding import PartitionSpec as P


def solve_users(normal_sum, right_side, number):
    width_rank = normal_sum.shape[-1]
    shifted = normal_sum + (0.1 * number / width_rank)[:, None, None] * jnp.eye(
        width_rank, dtype=jnp.float32
    )
    factor_low = jnp.linalg.cholesky(shifted)
    middle = jax.scipy.linalg.solve_triangular(factor_low, right_side[:, :, None], lower=True)
    answer = jax.scipy.linalg.solve_triangular(factor_low, middle, lower=True, trans=1)
    return answer[:, :, 0]


def per_device(item_factors, item_index, ratings, counts):
    item_block = lax.all_gather(item_factors, "col", axis=0, tiled=True)
    position = lax.broadcasted_iota(jnp.int32, item_index.shape, 1)
    live_slot = (position < counts).astype(jnp.bfloat16)
    chosen = jnp.take(item_block, item_index, axis=0)
    weighted = chosen * live_slot[:, :, None]
    scaled = ratings * live_slot
    moved_rows = lax.all_to_all(weighted, "row", split_axis=0, concat_axis=1, tiled=True)
    moved_scaled, moved_counts = (
        lax.all_to_all(scaled, "row", split_axis=0, concat_axis=1, tiled=True),
        lax.all_to_all(counts.astype(jnp.bfloat16), "row", split_axis=0, concat_axis=1, tiled=True),
    )
    normal_sum = jnp.einsum(
        "usa,usb->uab", moved_rows, moved_rows, preferred_element_type=jnp.float32
    )
    right_side = jnp.einsum(
        "us,usa->ua", moved_scaled, moved_rows, preferred_element_type=jnp.float32
    )
    number = jnp.sum(moved_counts.astype(jnp.float32), axis=1)
    answer = solve_users(normal_sum, right_side, number)
    return answer[None]


def solution(mesh):
    return jax.shard_map(
        per_device,
        mesh=mesh,
        in_specs=(P(("row", "col"), None), P("col", "row"), P("col", "row"), P("col", "row")),
        out_specs=P("col", "row", None),
        check_vma=False,
    )
```

profile of v0, /device:TPU:0, one launch (start us, length us, event | category | flops | bytes accessed | tf_op | source)
XLA Modules:
  0.0 328.6 jit_solution(2358926423072523534)
XLA Ops:
  0.0 0.7 convert_reduce_fusion.1
  0.7 0.7 all_to_all.47
  1.4 5.2 %all-to-all-start.1 = ((bf16[8,8,1]{1,2,0:T(2,128)(2,1)}), bf16[8,8,1]{1,2,0:T(2,128)(2,1)S(1)}, u32[]{:S(2)}, u32[]{:S(2)}) async-start(bf16[8,8,1]{1,2,0:T(2,128)(2,1)} %all_to_all.47), calls=%async_computation.1 | async-start | bytes 8192 | tf_op jit(solution)/shard_map/all_to_all | solution.py:28
  6.5 0.8 fusion.9
  7.4 0.9 compare_and_fusion
  8.2 0.7 fusion.7
  9.0 13.8 %all_gather.3 = bf16[512,128]{1,0:T(8,128)(2,1)S(1)} all-gather(bf16[128,128]{1,0:T(8,128)(2,1)} %param.4), channel_id=1, replica_groups=mesh['row'=8,'col'=4] {'col'}, dimensions={0}, use_global_device_ids=true | all-gather | bytes 163840 | tf_op jit(solution)/shard_map/all_gather | solution.py:19
  22.9 57.4 %gather_fusion = bf16[16384,128]{1,0:T(8,128)(2,1)} fusion(bf16[512,128]{1,0:T(8,128)(2,1)S(1)} %all_gather.3, s32[16384]{0:T(1024)S(1)} %broadcast_clamp_fusion), kind=kCustom, calls=%fused_computation | custom fusion | bytes 8454144 | tf_op jit(solution)/shard_map/jit(_take)/gather | solution.py:22
  80.2 7.6 %select_multiply_fusion = bf16[64,256,128]{2,1,0:T(8,128)(2,1)} fusion(bf16[64,256,128]{2,1,0:T(8,128)(2,1)} %bitcast.51, pred[64,256]{1,0:T(8,128)(4,1)S(1)} %compare_and_fusion, bf16[64,256]{1,0:T(8,128)(2,1)S(1)} %fusion.7), kind=kLoop, calls=%fused_computation.1 | loop fusion | flops 4194304 | bytes 8437760 | tf_op jit(solution)/shard_map/mul | solution.py:23
  87.8 0.0 copy-start.1
  87.8 0.0 copy-start.2
  87.8 0.0 all-to-all-done.1
  87.8 4.6 %all-to-all-start = ((bf16[64,256,128]{2,1,0:T(8,128)(2,1)}), bf16[64,256,128]{2,1,0:T(8,128)(2,1)}, u32[]{:S(2)}, u32[]{:S(2)}) async-start(bf16[64,256,128]{2,1,0:T(8,128)(2,1)} %select_multiply_fusion), calls=%async_computation | async-start | bytes 8388608 | tf_op jit(solution)/shard_map/all_to_all | solution.py:25
  92.4 0.0 copy-done.1
  92.5 0.0 copy-done.2
  92.5 0.7 fusion.10
  93.2 48.3 %all-to-all-done = bf16[64,256,128]{2,1,0:T(8,128)(2,1)} async-done(((bf16[64,256,128]{2,1,0:T(8,128)(2,1)}), bf16[64,256,128]{2,1,0:T(8,128)(2,1)}, u32[]{:S(2)}, u32[]{:S(2)}) %all-to-all-start) | async-done | bytes 4194336 | tf_op jit(solution)/shard_map/all_to_all | solution.py:25
  141.5 3.3 %all-to-all-start.2 = ((bf16[8,8,256]{2,1,0:T(8,128)(2,1)}), bf16[8,8,256]{2,1,0:T(8,128)(2,1)S(1)}, u32[]{:S(2)}, u32[]{:S(2)}) async-start(bf16[8,8,256]{2,1,0:T(8,128)(2,1)} %fusion.10), calls=%async_computation.2 | async-start | bytes 65536 | tf_op jit(solution)/shard_map/all_to_all | solution.py:27
  144.8 2.5 copy.14
  147.3 0.0 copy-start
  147.3 1.9 copy-done
  149.2 1.4 fusion.12
  150.6 0.2 copy.17
  150.8 0.2 fusion.4
  151.0 93.8 %custom-call.11 = f32[8,128,128]{2,1,0:T(8,128)S(1)} custom-call(f32[8,128,128]{2,1,0:T(8,128)S(1)} %fusion.4), custom_call_target="Cholesky" | custom-call | tf_op jit(solution)/shard_map/jit(cholesky)/cholesky | solution.py:12
  244.8 0.1 select_reduce_fusion
  244.8 0.1 compare_reduce_fusion
  244.9 0.1 select_bitcast_fusion
  245.1 78.6 %custom-call.12 = f32[8,1,128,128]{2,3,1,0:T(8,128)S(1)} custom-call(f32[8,1,128,128]{3,2,1,0:T(8,128)S(1)} %select_bitcast_fusion), custom_call_target="InvertDiagBlocksLowerTriangular" | custom-call | tf_op jit(solution)/shard_map/jit(_solve_triangular)/vmap()/triangular_solve | solution.py:14
  323.7 0.0 all-to-all-done.2
  323.7 2.8 convolution_bitcast_fusion
  326.5 0.6 convolution_bitcast_fusion.1
  327.1 1.5 fusion
  (7 shorter events, 0.1 us)
Async XLA Ops:
  1.4 86.4 %all-to-all-start.1 = ((bf16[8,8,1]{1,2,0:T(2,128)(2,1)}), bf16[8,8,1]{1,2,0:T(2,128)(2,1)S(1)}, u32[]{:S(2)}, u32[]{:S(2)}) async-start(bf16[8,8,1]{1,2,0:T(2,128)(2,1)} %all_to_all.47), calls=%async_computation.1 | async-start | bytes 8192 | tf_op jit(solution)/shard_map/all_to_all | solution.py:28
  87.8 4.7 %copy-start.1 = (bf16[64,256]{1,0:T(8,128)(2,1)S(1)}, bf16[64,256]{1,0:T(8,128)(2,1)}, u32[]{:S(2)}) copy-start(bf16[64,256]{1,0:T(8,128)(2,1)} %param.6) | copy-start | bytes 98308
  87.8 4.7 %copy-start.2 = (s32[64,1]{0,1:T(1,128)S(1)}, s32[64,1]{0,1:T(1,128)}, u32[]{:S(2)}) copy-start(s32[64,1]{0,1:T(1,128)} %param.7) | copy-start | bytes 772
  87.8 53.7 %all-to-all-start = ((bf16[64,256,128]{2,1,0:T(8,128)(2,1)}), bf16[64,256,128]{2,1,0:T(8,128)(2,1)}, u32[]{:S(2)}, u32[]{:S(2)}) async-start(bf16[64,256,128]{2,1,0:T(8,128)(2,1)} %select_multiply_fusion), calls=%async_computation | async-start | bytes 8388608 | tf_op jit(solution)/shard_map/all_to_all | solution.py:25
  141.5 182.2 %all-to-all-start.2 = ((bf16[8,8,256]{2,1,0:T(8,128)(2,1)}), bf16[8,8,256]{2,1,0:T(8,128)(2,1)S(1)}, u32[]{:S(2)}, u32[]{:S(2)}) async-start(bf16[8,8,256]{2,1,0:T(8,128)(2,1)} %fusion.10), calls=%async_computation.2 | async-start | bytes 65536 | tf_op jit(solution)/shard_map/all_to_all | solution.py:27
  147.3 1.9 copy-start
where the time goes:
time: 329 us
  other arithmetic  184 us (56%)
  local copies, waits for them, and re-layouts  62.7 us (19%)
  waiting for transfers between devices  48.3 us (15%)
  blocking collectives  13.8 us (4%)
  starting transfers between devices  13.1 us (4%)
  matrix products  6.29 us (2%)
    another operation x4, other arithmetic, solve_users(): factor_low = jnp.linalg.cholesky(shifted)  94 us
    another operation x3, other arithmetic, solve_users(): jax.scipy.linalg.solve_triangular(factor_low, middle, lower=True, trans=1)  78.7 us
    gather x1, local copies, waits for them, and re-layouts, per_device(): chosen = jnp.take(item_block, item_index, axis=0)  57.4 us
    all_to_all x1, waiting for transfers between devices, per_device(): lax.all_to_all(weighted, 'row', split_axis=0, concat_axis=1, tiled=True)  48.3 us
    all_gather x1, blocking collectives, per_device(): item_block = lax.all_gather(item_factors, 'col', axis=0, tiled=True)  13.8 us
    mul x1, other arithmetic, per_device(): weighted = chosen * live_slot[:, :, None]  7.56 us
  transfers between devices with their start and end apart: 3, of which 1 were waited for; matrix products, arithmetic and copies ran while one was open for 75% of the time, Pallas kernels for 0%

commit v1 on v0

v1 whole, which is shorter than its diff:
```python
import functools

import jax
import jax.numpy as jnp
from jax import lax
from jax.experimental import pallas as pl
from jax.experimental.pallas import tpu as pltpu
from jax.sharding import PartitionSpec as P

PANEL = 8
TILE = 256


def lane(x, i):
    where = jnp.full(x.shape, i, jnp.int32)
    return jnp.take_along_axis(x, where, axis=1, mode="promise_in_bounds")


def factor_and_solve(a_ref, l_ref, y, shift, users, rank):
    lanes = lax.broadcasted_iota(jnp.int32, (users, rank), 1)

    def slab(i):
        return pl.ds(pl.multiple_of(i * users, users), users)

    def panel(b, carry):
        y, inv_diag = carry
        i0 = b * PANEL
        rows = []
        for t in range(PANEL):
            rows.append(a_ref[slab(i0 + t), :] + jnp.where(lanes == i0 + t, shift, 0.0))
        right, low = [], []
        for t in range(PANEL):
            i = i0 + t
            inv = 1.0 / lane(rows[t], i)
            upper = jnp.where(lanes > i, rows[t], 0.0)
            scaled = upper * inv
            for t2 in range(t + 1, PANEL):
                rows[t2] = rows[t2] - lane(scaled, i0 + t2) * upper
            y = y - lane(y, i) * scaled
            inv_diag = jnp.where(lanes == i, inv, inv_diag)
            l_ref[slab(i), :] = jnp.where(lanes < i, rows[t], 0.0)
            right.append(upper)
            low.append(scaled)

        def trailing(g, _):
            for r in range(PANEL):
                j = g * PANEL + r
                acc = a_ref[slab(j), :]
                for t in range(PANEL):
                    acc = acc - lane(low[t], j) * right[t]
                a_ref[slab(j), :] = acc
            return 0

        lax.fori_loop(b + 1, rank // PANEL, trailing, 0)
        return y, inv_diag

    y, inv_diag = lax.fori_loop(0, rank // PANEL, panel, (y, jnp.zeros_like(y)))

    def back(b, x):
        for r in range(PANEL):
            j = rank - 1 - (b * PANEL + r)
            x = x - lane(x, j) * (l_ref[slab(j), :] * inv_diag)
        return x

    return lax.fori_loop(0, rank // PANEL, back, y * inv_diag)


def kernel(item_ref, slot_ref, out_ref, x_ref, a_ref, l_ref):
    n_block, items, rank = item_ref.shape
    users, slots = slot_ref.shape[1], slot_ref.shape[2] // 3
    halves = items // TILE
    pad = x_ref.shape[1] - rank
    entry = lax.broadcasted_iota(jnp.int32, (TILE, slots), 0).astype(jnp.float32)
    first = lax.broadcasted_iota(jnp.int32, (pad, slots), 0) == 0

    def block(k, number):
        table = item_ref[k].T
        left = jnp.concatenate([table[:, h * TILE : (h + 1) * TILE] for h in range(halves)], axis=0)
        packed = slot_ref[k].astype(jnp.float32)
        low, high, rate = packed[:, :slots], packed[:, slots : 2 * slots], packed[:, 2 * slots :]
        here = pl.ds(pl.multiple_of(k * slots, slots), slots)
        for u in range(users):
            hot = (entry == low[u : u + 1]).astype(jnp.bfloat16)
            picked = jnp.dot(left, hot, preferred_element_type=jnp.float32)
            rows = jnp.zeros((rank, slots), jnp.float32)
            for h in range(halves):
                rows = jnp.where(high[u : u + 1] == h, picked[h * rank : (h + 1) * rank], rows)
            x_ref[u, 0:rank, here] = rows.astype(jnp.bfloat16)
            x_ref[u, rank:, here] = jnp.where(first, rate[u : u + 1], 0.0).astype(jnp.bfloat16)
        return number + jnp.sum((high >= 0).astype(jnp.float32), axis=1, keepdims=True)

    number = lax.fori_loop(0, n_block, block, jnp.zeros((users, 1), jnp.float32))
    for u in range(users):
        full = lax.dot_general(
            x_ref[u], x_ref[u, 0:rank, :], (((1,), (1,)), ((), ())), preferred_element_type=jnp.float32
        )
        a_ref[pl.ds(u, rank + 8, stride=users), :] = full[: rank + 8]
    y = a_ref[rank * users : (rank + 1) * users, :]
    out_ref[...] = factor_and_solve(a_ref, l_ref, y, 0.1 * number / rank, users, rank)


def solve(items, slots_in, rank):
    n_block, users, width = slots_in.shape
    return pl.pallas_call(
        kernel,
        out_shape=jax.ShapeDtypeStruct((users, rank), jnp.float32),
        in_specs=[pl.BlockSpec(memory_space=pltpu.VMEM)] * 2,
        out_specs=pl.BlockSpec(memory_space=pltpu.VMEM),
        scratch_shapes=[
            pltpu.VMEM((users, rank + 16, n_block * width // 3), jnp.bfloat16),
            pltpu.VMEM(((rank + 8) * users, rank), jnp.float32),
            pltpu.VMEM((rank * users, rank), jnp.float32),
        ],
        compiler_params=pltpu.CompilerParams(vmem_limit_bytes=48 * 1024 * 1024),
    )(items, slots_in)


def per_device(n_row, item_factors, item_index, ratings, counts):
    rank = item_factors.shape[1]
    users, slots = item_index.shape
    items = lax.all_gather(item_factors, ("row", "col"), axis=0, tiled=True)
    items = items.reshape(n_row, -1, rank)
    live = lax.broadcasted_iota(jnp.int32, item_index.shape, 1) < counts
    low = (item_index % TILE).astype(jnp.bfloat16)
    high = jnp.where(live, item_index // TILE, -1).astype(jnp.bfloat16)
    packed = jnp.concatenate([low, high, ratings], axis=1).reshape(n_row, users // n_row, 3 * slots)
    moved = lax.all_to_all(packed, "row", split_axis=0, concat_axis=0, tiled=True)
    return solve(items, moved, rank)[None]


def solution(mesh):
    return jax.shard_map(
        functools.partial(per_device, mesh.shape["row"]),
        mesh=mesh,
        in_specs=(P(("row", "col"), None), P("col", "row"), P("col", "row"), P("col", "row")),
        out_specs=P("col", "row", None),
        check_vma=False,
    )
```

time: 329 us -> 129 us (0.39)
  other arithmetic: 184 us -> 0.93 us
  local copies, waits for them, and re-layouts: 62.7 us -> 1.88 us
  Pallas kernels: 0 us -> 54.2 us
  between operations: 0.16 us -> 13.4 us
  starting transfers between devices: 13.1 us -> 0.01 us
  matrix products: 6.29 us -> 0 us
  blocking collectives: 13.8 us -> 10.2 us
    another operation x7 -> x0, other arithmetic: 173 us -> none  [the longest x4 94 us: solve_users(): factor_low = jnp.linalg.cholesky(shifted)]
    gather x1 -> x0, local copies, waits for them, and re-layouts: 57.4 us -> none  [per_device(): chosen = jnp.take(item_block, item_index, axis=0)]
    pallas_call x0 -> x1, Pallas kernels: none -> 54.2 us  [solve(): pl.pallas_call(kernel, out_shape=jax.ShapeDtypeStruct((users, rank), jnp....]
    all_to_all x3 -> x0, waiting for transfers between devices: 48.3 us -> none  [the longest x1 48.3 us: per_device(): lax.all_to_all(weighted, 'row', split_axis=0, concat_axis=1, tiled=True)]
    all_gather x0 -> x1, waiting for transfers between devices: none -> 47.8 us  [per_device(): items = lax.all_gather(item_factors, ('row', 'col'), axis=0, tiled=True)]
    all_gather x1 -> x0, blocking collectives: 13.8 us -> none  [per_device(): item_block = lax.all_gather(item_factors, 'col', axis=0, tiled=True)]
    all_to_all x3 -> x0, starting transfers between devices: 13.1 us -> none  [the longest x1 5.17 us: per_device(): lax.all_to_all(counts.astype(jnp.bfloat16), 'row', split_axis=0, concat_a...]
    all_to_all x0 -> x1, blocking collectives: none -> 10.2 us  [per_device(): lax.all_to_all(packed, 'row', split_axis=0, concat_axis=0, tiled=True)]
  transfers between devices with their start and end apart: 3 -> 1, of which waited for: 1 -> 1; matrix products, arithmetic and copies ran while one was open for 75% -> 1% of each run, Pallas kernels for 0% -> 0%
where the time goes in v1:
time: 129 us
  Pallas kernels  54.2 us (42%)
  waiting for transfers between devices  48.5 us (38%)
  between operations  13.4 us (10%)
  blocking collectives  10.2 us (8%)
  local copies, waits for them, and re-layouts  1.88 us (1%)
    pallas_call x1, Pallas kernels, solve(): pl.pallas_call(kernel, out_shape=jax.ShapeDtypeStruct((users, rank), jnp....  54.2 us
    all_gather x1, waiting for transfers between devices, per_device(): items = lax.all_gather(item_factors, ('row', 'col'), axis=0, tiled=True)  47.8 us
    all_to_all x1, blocking collectives, per_device(): lax.all_to_all(packed, 'row', split_axis=0, concat_axis=0, tiled=True)  10.2 us
  transfers between devices with their start and end apart: 1, of which 1 were waited for; matrix products, arithmetic and copies ran while one was open for 1% of the time, Pallas kernels for 0%

profile of v1, /device:TPU:0, one launch (start us, length us, event | category | flops | bytes accessed | tf_op | source)
XLA Modules:
  0.0 129.1 jit_solution(14573536707368055995)
XLA Ops:
  6.5 0.0 all-gather.2.cloned.1.call-start
  6.5 0.7 all-gather.2.cloned.1.call-update
  7.3 0.0 copy-start.2
  7.3 0.6 copy-done.2
  7.9 0.0 copy-start.1
  7.9 0.9 fusion
  8.8 0.0 copy-done.1
  8.9 10.2 %all_to_all.5.slot_ref = bf16[8,8,768]{2,1,0:T(8,128)(2,1)S(1)} all-to-all(bf16[8,8,768]{2,1,0:T(8,128)(2,1)S(1)} %maximum_bitcast_fusion), channel_id=1, replica_groups=mesh['row'=8,'col'=4] {'row'}, dimensions={0} | all-to-all | bytes 196608 | tf_op jit(solution)/shard_map/all_to_all | solution.py:127
  19.0 47.8 %all-gather.2.cloned.1.call-done = bf16[4096,128]{1,0:T(8,128)(2,1)} async-done(((bf16[128,128]{1,0:T(8,128)(2,1)}), bf16[4096,128]{1,0:T(8,128)(2,1)}) %all-gather.2.cloned.1.call-update) | async-done | bytes 1048592 | tf_op jit(solution)/shard_map/all_gather | solution.py:121
  66.8 0.0 copy-start
  66.8 1.2 copy-done
  68.1 54.2 %shard_map.46 = f32[8,128]{1,0:T(8,128)} custom-call(bf16[8,512,128]{2,1,0:T(8,128)(2,1)S(1)} %bitcast.5, bf16[8,8,768]{2,1,0:T(8,128)(2,1)S(1)} %all_to_all.5.slot_ref), custom_call_target="tpu_custom_call" | custom-call | tf_op jit(solution)/shard_map/pallas_call | solution.py:104
  (1 shorter events, 0.0 us)
Async XLA Ops:
  6.5 60.3 %all-gather.2.cloned.1.call-start = ((), (), s32[]{:S(2)}) async-start(), calls=%async_computation.1 | async-start | bytes 1081344 | tf_op jit(solution)/shard_map/all_gather | solution.py:121
  7.3 0.7 copy-start.2
  7.9 0.9 copy-start.1
  66.8 1.2 copy-start
Sparse Core Ops, SparseCore 0:
  10.3 56.4 all-gather.1

commit v2 on v1

--- a/solution.py
+++ b/solution.py
@@ -8,6 +8,7 @@
 from jax.sharding import PartitionSpec as P
 
 PANEL = 8
+GROUP = 32
 TILE = 256
 
 
@@ -16,29 +17,38 @@
     return jnp.take_along_axis(x, where, axis=1, mode="promise_in_bounds")
 
 
-def factor_and_solve(a_ref, l_ref, y, shift, users, rank):
+def factor_and_solve(a_ref, l_ref, s_ref, y, shift, users, rank):
     lanes = lax.broadcasted_iota(jnp.int32, (users, rank), 1)
 
     def slab(i):
         return pl.ds(pl.multiple_of(i * users, users), users)
 
-    def panel(b, carry):
+    def panel(first, last, b, carry):
         y, inv_diag = carry
         i0 = b * PANEL
         rows = []
         for t in range(PANEL):
             rows.append(a_ref[slab(i0 + t), :] + jnp.where(lanes == i0 + t, shift, 0.0))
+        small = {(t, t2): lane(rows[t], i0 + t2) for t in range(PANEL) for t2 in range(t, PANEL)}
+        side = [lane(y, i0 + t) for t in range(PANEL)]
         right, low = [], []
         for t in range(PANEL):
             i = i0 + t
-            inv = 1.0 / lane(rows[t], i)
+            inv = 1.0 / small[t, t]
+            for t2 in range(t + 1, PANEL):
+                ratio = small[t, t2] * inv
+                side[t2] = side[t2] - side[t] * ratio
+                for t3 in range(t2, PANEL):
+                    small[t2, t3] = small[t2, t3] - ratio * small[t, t3]
             upper = jnp.where(lanes > i, rows[t], 0.0)
             scaled = upper * inv
             for t2 in range(t + 1, PANEL):
-                rows[t2] = rows[t2] - lane(scaled, i0 + t2) * upper
-            y = y - lane(y, i) * scaled
+                rows[t2] = rows[t2] - small[t, t2] * scaled
+            y = y - side[t] * scaled
             inv_diag = jnp.where(lanes == i, inv, inv_diag)
             l_ref[slab(i), :] = jnp.where(lanes < i, rows[t], 0.0)
+            s_ref[0, slab(i - first * PANEL), :] = scaled
+            s_ref[1, slab(i - first * PANEL), :] = upper
             right.append(upper)
             low.append(scaled)
 
@@ -51,21 +61,39 @@
                 a_ref[slab(j), :] = acc
             return 0
 
-        lax.fori_loop(b + 1, rank // PANEL, trailing, 0)
+        lax.fori_loop(b + 1, last, trailing, 0)
         return y, inv_diag
 
-    y, inv_diag = lax.fori_loop(0, rank // PANEL, panel, (y, jnp.zeros_like(y)))
+    carry = (y, jnp.zeros_like(y))
+    step = GROUP // PANEL
+    for q in range(rank // GROUP):
+        carry = lax.fori_loop(q * step, (q + 1) * step, functools.partial(panel, q * step, (q + 1) * step), carry)
+        done = (q + 1) * GROUP
+        if done < rank:
+            for u in range(users):
+                mine = pl.ds(u, GROUP, stride=users)
+                left = s_ref[0, mine, :].T[done:]
+                update = jnp.dot(
+                    left, s_ref[1, mine, :], precision=lax.Precision.HIGHEST, preferred_element_type=jnp.float32
+                )
+                rest = pl.ds(done * users + u, rank - done, stride=users)
+                a_ref[rest, :] = a_ref[rest, :] - update
+    y, inv_diag = carry
 
     def back(b, x):
+        j0 = rank - 1 - b * PANEL
+        rows = [l_ref[slab(j0 - r), :] * inv_diag for r in range(PANEL)]
+        part = [lane(x, j0 - r) for r in range(PANEL)]
         for r in range(PANEL):
-            j = rank - 1 - (b * PANEL + r)
-            x = x - lane(x, j) * (l_ref[slab(j), :] * inv_diag)
+            for r2 in range(r + 1, PANEL):
+                part[r2] = part[r2] - part[r] * lane(rows[r], j0 - r2)
+            x = x - part[r] * rows[r]
         return x
 
     return lax.fori_loop(0, rank // PANEL, back, y * inv_diag)
 
 
-def kernel(item_ref, slot_ref, out_ref, x_ref, a_ref, l_ref):
+def kernel(item_ref, slot_ref, out_ref, x_ref, a_ref, l_ref, s_ref):
     n_block, items, rank = item_ref.shape
     users, slots = slot_ref.shape[1], slot_ref.shape[2] // 3
     halves = items // TILE
@@ -96,7 +124,7 @@
         )
         a_ref[pl.ds(u, rank + 8, stride=users), :] = full[: rank + 8]
     y = a_ref[rank * users : (rank + 1) * users, :]
-    out_ref[...] = factor_and_solve(a_ref, l_ref, y, 0.1 * number / rank, users, rank)
+    out_ref[...] = factor_and_solve(a_ref, l_ref, s_ref, y, 0.1 * number / rank, users, rank)
 
 
 def solve(items, slots_in, rank):
@@ -110,27 +138,129 @@
             pltpu.VMEM((users, rank + 16, n_block * width // 3), jnp.bfloat16),
             pltpu.VMEM(((rank + 8) * users, rank), jnp.float32),
             pltpu.VMEM((rank * users, rank), jnp.float32),
+            pltpu.VMEM((2, GROUP * users, rank), jnp.float32),
         ],
         compiler_params=pltpu.CompilerParams(vmem_limit_bytes=48 * 1024 * 1024),
     )(items, slots_in)
 
 
-def per_device(n_row, item_factors, item_index, ratings, counts):
+def exchange_kernel(n_row, n_col, item_ref, slot_ref, all_ref, got_ref, own_sem, z_sem, far_sem, near_sem, slot_sem):
+    row, col = lax.axis_index("row"), lax.axis_index("col")
+    half = n_row // 2
+    twin = row + 1 - 2 * lax.rem(row, 2)
+
+    def col_at(d):
+        return lax.rem(col + d, n_col)
+
+    def row_at(d):
+        return lax.rem(row + d, n_row)
+
+    def far(d):
+        return lax.rem(row + 2 * d, n_row)
+
+    barrier = pltpu.get_barrier_semaphore()
+    for d in range(1, n_col):
+        pl.semaphore_signal(barrier, inc=1, device_id=(row, col_at(d)), device_id_type=pl.DeviceIdType.MESH)
+    for d in range(1, n_row):
+        pl.semaphore_signal(barrier, inc=1, device_id=(row_at(d), col), device_id_type=pl.DeviceIdType.MESH)
+
+    own_items = pltpu.make_async_copy(item_ref, all_ref.at[row, col], own_sem.at[0])
+    own_items.start()
+    own_slots = pltpu.make_async_copy(slot_ref.at[row], got_ref.at[row], own_sem.at[1])
+    own_slots.start()
+    pl.semaphore_wait(barrier, n_col + n_row - 2)
+
+    def send(src, dst, sems, where):
+        copy = pltpu.make_async_remote_copy(
+            src_ref=src,
+            dst_ref=dst,
+            send_sem=sems[0],
+            recv_sem=sems[1],
+            device_id=where,
+            device_id_type=pl.DeviceIdType.MESH,
+        )
+        copy.start()
+        return copy
+
+    along = {}
+    for d in range(1, n_col):
+        sems = z_sem.at[0, d], z_sem.at[1, d]
+        along[d] = send(item_ref, all_ref.at[row, col], sems, (row, col_at(d)))
+    across, pair = {}, {}
+
+    def spread(d, src):
+        piece = lax.rem(col - d + n_col, n_col)
+        for e in range(1, half):
+            sems = far_sem.at[0, d, e], far_sem.at[1, d, e]
+            across[d, e] = send(src, all_ref.at[row, piece], sems, (far(e), col))
+        sems = near_sem.at[0, d, 0], near_sem.at[1, d, 0]
+        pair[d, 0] = send(src, all_ref.at[row, piece], sems, (twin, col))
+
+    spread(0, item_ref)
+    slots = []
+    for d in range(1, n_row):
+        to = row_at(d)
+        slots.append(send(slot_ref.at[to], got_ref.at[row], (slot_sem.at[0, d], slot_sem.at[1, d]), (to, col)))
+    for d in range(1, n_col):
+        along[d].wait_recv()
+        spread(d, all_ref.at[row, lax.rem(col - d + n_col, n_col)])
+    for d in range(n_col):
+        piece = lax.rem(col - d + n_col, n_col)
+        for e in range(1, half):
+            across[d, e].wait_recv()
+            source = lax.rem(row - 2 * e + n_row, n_row)
+            sems = near_sem.at[0, d, e], near_sem.at[1, d, e]
+            pair[d, e] = send(all_ref.at[source, piece], all_ref.at[source, piece], sems, (twin, col))
+    for copy in slots:
+        copy.wait()
+    for copy in along.values():
+        copy.wait_send()
+    for copy in across.values():
+        copy.wait_send()
+    for copy in pair.values():
+        copy.wait()
+    own_items.wait()
+    own_slots.wait()
+
+
+def exchange(n_row, n_col, items, packed):
+    half = n_row // 2
+    vmem = pl.BlockSpec(memory_space=pltpu.VMEM)
+    return pl.pallas_call(
+        functools.partial(exchange_kernel, n_row, n_col),
+        out_shape=(
+            jax.ShapeDtypeStruct((n_row, n_col) + items.shape, items.dtype),
+            jax.ShapeDtypeStruct(packed.shape, packed.dtype),
+        ),
+        in_specs=[vmem] * 2,
+        out_specs=(vmem, vmem),
+        scratch_shapes=[
+            pltpu.SemaphoreType.DMA((2,)),
+            pltpu.SemaphoreType.DMA((2, n_col)),
+            pltpu.SemaphoreType.DMA((2, n_col, half)),
+            pltpu.SemaphoreType.DMA((2, n_col, half)),
+            pltpu.SemaphoreType.DMA((2, n_row)),
+        ],
+        compiler_params=pltpu.CompilerParams(
+            collective_id=0, has_side_effects=True, vmem_limit_bytes=24 * 1024 * 1024
+        ),
+    )(items, packed)
+
+
+def per_device(n_row, n_col, item_factors, item_index, ratings, counts):
     rank = item_factors.shape[1]
     users, slots = item_index.shape
-    items = lax.all_gather(item_factors, ("row", "col"), axis=0, tiled=True)
-    items = items.reshape(n_row, -1, rank)
     live = lax.broadcasted_iota(jnp.int32, item_index.shape, 1) < counts
     low = (item_index % TILE).astype(jnp.bfloat16)
     high = jnp.where(live, item_index // TILE, -1).astype(jnp.bfloat16)
     packed = jnp.concatenate([low, high, ratings], axis=1).reshape(n_row, users // n_row, 3 * slots)
-    moved = lax.all_to_all(packed, "row", split_axis=0, concat_axis=0, tiled=True)
-    return solve(items, moved, rank)[None]
+    items, moved = exchange(n_row, n_col, item_factors, packed)
+    return solve(items.reshape(n_row, -1, rank), moved, rank)[None]
 
 
 def solution(mesh):
     return jax.shard_map(
-        functools.partial(per_device, mesh.shape["row"]),
+        functools.partial(per_device, mesh.shape["row"], mesh.shape["col"]),
         mesh=mesh,
         in_specs=(P(("row", "col"), None), P("col", "row"), P("col", "row"), P("col", "row")),
         out_specs=P("col", "row", None),

time: 129 us -> 35.7 us (0.28)
  waiting for transfers between devices: 48.5 us -> 0 us
  Pallas kernels: 54.2 us -> 33.1 us
  between operations: 13.4 us -> 0.04 us
  blocking collectives: 10.2 us -> 0 us
    all_gather x1 -> x0, waiting for transfers between devices: 47.8 us -> none  [per_device(): items = lax.all_gather(item_factors, ('row', 'col'), axis=0, tiled=True)]
    pallas_call x1, Pallas kernels: 54.2 us -> 16.9 us  [solve(): pl.pallas_call(kernel, out_shape=jax.ShapeDtypeStruct((users, rank), jnp....]
    pallas_call x0 -> x1, Pallas kernels: none -> 16.1 us  [exchange(): pl.pallas_call(functools.partial(exchange_kernel, n_row, n_col), out_shap...]
    all_to_all x1 -> x0, blocking collectives: 10.2 us -> none  [per_device(): lax.all_to_all(packed, 'row', split_axis=0, concat_axis=0, tiled=True)]
  transfers between devices with their start and end apart: 1 -> 0, of which waited for: 1 -> 0; matrix products, arithmetic and copies ran while one was open for 1% -> 0% of each run, Pallas kernels for 0% -> 0%
where the time goes in v2:
time: 35.7 us; the launch traced here: 35.4 us
  Pallas kernels  33.1 us (93%)
  local copies, waits for them, and re-layouts  1.39 us (4%)
  other arithmetic  0.93 us (3%)
    pallas_call x1, Pallas kernels, solve(): pl.pallas_call(kernel, out_shape=jax.ShapeDtypeStruct((users, rank), jnp....  16.9 us
    pallas_call x1, Pallas kernels, exchange(): pl.pallas_call(functools.partial(exchange_kernel, n_row, n_col), out_shap...  16.1 us
    unnamed x6, local copies, waits for them, and re-layouts  1.39 us
    convert_element_type x1, other arithmetic, per_device(): low = (item_index % TILE).astype(jnp.bfloat16)  0.93 us

profile of v2, /device:TPU:0, one launch (start us, length us, event | category | flops | bytes accessed | tf_op | source)
XLA Modules:
  0.0 35.4 jit_solution(13040372889136710714)
XLA Ops:
  0.0 0.0 copy-start.2
  0.0 0.7 %copy-done.2 = s32[64,1]{0,1:T(1,128)S(1)} copy-done((s32[64,1]{0,1:T(1,128)S(1)}, s32[64,1]{0,1:T(1,128)}, u32[]{:S(2)}) %copy-start.2) | copy-done | bytes 280
  0.7 0.0 copy-start.1
  0.7 0.9 %fusion = (bf16[64,256]{1,0:T(8,128)(2,1)S(1)}, bf16[64,256]{1,0:T(8,128)(2,1)S(1)}) fusion(s32[64,256]{1,0:T(8,128)} %param.5, s32[64]{0:T(128)S(1)} %bitcast.6), kind=kLoop, calls=%fused_computation.6 | loop fusion | flops 376832 | bytes 131328 | tf_op jit(solution)/shard_map/convert_element_type | solution.py:254
  1.6 0.0 copy-done.1
  1.6 0.0 copy-start
  1.6 0.7 %copy-done = bf16[128,128]{1,0:T(8,128)(2,1)S(1)} copy-done((bf16[128,128]{1,0:T(8,128)(2,1)S(1)}, bf16[128,128]{1,0:T(8,128)(2,1)}, u32[]{:S(2)}) %copy-start) | copy-done | bytes 32792
  2.4 16.1 %shard_map.46 = (bf16[8,4,128,128]{3,2,1,0:T(8,128)(2,1)S(1)}, bf16[8,8,768]{2,1,0:T(8,128)(2,1)S(1)}) custom-call(bf16[128,128]{1,0:T(8,128)(2,1)S(1)} %copy-done, bf16[8,8,768]{2,1,0:T(8,128)(2,1)S(1)} %maximum_bitcast_fusion.slot_ref), custom_call_target="tpu_custom_call" | custom-call | tf_op jit(solution)/shard_map/pallas_call | solution.py:229
  18.5 16.9 %shard_map.47 = f32[8,128]{1,0:T(8,128)} custom-call(bf16[8,512,128]{2,1,0:T(8,128)(2,1)S(1)} %bitcast.5, bf16[8,8,768]{2,1,0:T(8,128)(2,1)S(1)} %get-tuple-element.8.slot_ref), custom_call_target="tpu_custom_call" | custom-call | tf_op jit(solution)/shard_map/pallas_call | solution.py:132
  (1 shorter events, 0.0 us)
Async XLA Ops:
  0.0 0.7 %copy-start.2 = (s32[64,1]{0,1:T(1,128)S(1)}, s32[64,1]{0,1:T(1,128)}, u32[]{:S(2)}) copy-start(s32[64,1]{0,1:T(1,128)} %param.7) | copy-start | bytes 772
  0.7 0.9 %copy-start.1 = (bf16[64,256]{1,0:T(8,128)(2,1)S(1)}, bf16[64,256]{1,0:T(8,128)(2,1)}, u32[]{:S(2)}) copy-start(bf16[64,256]{1,0:T(8,128)(2,1)} %param.6) | copy-start | bytes 98308
  1.6 0.8 %copy-start = (bf16[128,128]{1,0:T(8,128)(2,1)S(1)}, bf16[128,128]{1,0:T(8,128)(2,1)}, u32[]{:S(2)}) copy-start(bf16[128,128]{1,0:T(8,128)(2,1)} %item_ref.1) | copy-start | bytes 98308

commit v3 on v2

--- a/solution.py
+++ b/solution.py
@@ -8,7 +8,7 @@
 from jax.sharding import PartitionSpec as P
 
 PANEL = 8
-GROUP = 32
+GROUP = 16
 TILE = 256
 
 
@@ -93,58 +93,57 @@
     return lax.fori_loop(0, rank // PANEL, back, y * inv_diag)
 
 
-def kernel(item_ref, slot_ref, out_ref, x_ref, a_ref, l_ref, s_ref):
-    n_block, items, rank = item_ref.shape
-    users, slots = slot_ref.shape[1], slot_ref.shape[2] // 3
-    halves = items // TILE
-    pad = x_ref.shape[1] - rank
-    entry = lax.broadcasted_iota(jnp.int32, (TILE, slots), 0).astype(jnp.float32)
-    first = lax.broadcasted_iota(jnp.int32, (pad, slots), 0) == 0
-
-    def block(k, number):
-        table = item_ref[k].T
-        left = jnp.concatenate([table[:, h * TILE : (h + 1) * TILE] for h in range(halves)], axis=0)
-        packed = slot_ref[k].astype(jnp.float32)
-        low, high, rate = packed[:, :slots], packed[:, slots : 2 * slots], packed[:, 2 * slots :]
-        here = pl.ds(pl.multiple_of(k * slots, slots), slots)
-        for u in range(users):
-            hot = (entry == low[u : u + 1]).astype(jnp.bfloat16)
-            picked = jnp.dot(left, hot, preferred_element_type=jnp.float32)
-            rows = jnp.zeros((rank, slots), jnp.float32)
-            for h in range(halves):
-                rows = jnp.where(high[u : u + 1] == h, picked[h * rank : (h + 1) * rank], rows)
-            x_ref[u, 0:rank, here] = rows.astype(jnp.bfloat16)
-            x_ref[u, rank:, here] = jnp.where(first, rate[u : u + 1], 0.0).astype(jnp.bfloat16)
-        return number + jnp.sum((high >= 0).astype(jnp.float32), axis=1, keepdims=True)
-
-    number = lax.fori_loop(0, n_block, block, jnp.zeros((users, 1), jnp.float32))
+def solve_kernel(full_ref, number_ref, out_ref, a_ref, l_ref, s_ref):
+    users, rank = out_ref.shape
     for u in range(users):
-        full = lax.dot_general(
-            x_ref[u], x_ref[u, 0:rank, :], (((1,), (1,)), ((), ())), preferred_element_type=jnp.float32
-        )
-        a_ref[pl.ds(u, rank + 8, stride=users), :] = full[: rank + 8]
+        a_ref[pl.ds(u, rank + 8, stride=users), :] = full_ref[u, : rank + 8]
     y = a_ref[rank * users : (rank + 1) * users, :]
-    out_ref[...] = factor_and_solve(a_ref, l_ref, s_ref, y, 0.1 * number / rank, users, rank)
-
-
-def solve(items, slots_in, rank):
-    n_block, users, width = slots_in.shape
+    out_ref[...] = factor_and_solve(a_ref, l_ref, s_ref, y, 0.1 * number_ref[...] / rank, users, rank)
+
+
+def solve(full, number):
+    users, rank = number.shape
     return pl.pallas_call(
-        kernel,
+        solve_kernel,
         out_shape=jax.ShapeDtypeStruct((users, rank), jnp.float32),
         in_specs=[pl.BlockSpec(memory_space=pltpu.VMEM)] * 2,
         out_specs=pl.BlockSpec(memory_space=pltpu.VMEM),
         scratch_shapes=[
-            pltpu.VMEM((users, rank + 16, n_block * width // 3), jnp.bfloat16),
             pltpu.VMEM(((rank + 8) * users, rank), jnp.float32),
             pltpu.VMEM((rank * users, rank), jnp.float32),
             pltpu.VMEM((2, GROUP * users, rank), jnp.float32),
         ],
-        compiler_params=pltpu.CompilerParams(vmem_limit_bytes=48 * 1024 * 1024),
-    )(items, slots_in)
-
-
-def exchange_kernel(n_row, n_col, item_ref, slot_ref, all_ref, got_ref, own_sem, z_sem, far_sem, near_sem, slot_sem):
+        compiler_params=pltpu.CompilerParams(vmem_limit_bytes=16 * 1024 * 1024),
+    )(full, number)
+
+
+def place_block(items_ref, slot_ref, x_ref, k, number):
+    n_col, depth, rank = items_ref.shape[1:]
+    users, slots = slot_ref.shape[1], slot_ref.shape[2] // 3
+    halves = n_col * depth // TILE
+    pad = x_ref.shape[1] - rank
+    entry = lax.broadcasted_iota(jnp.int32, (TILE, slots), 0).astype(jnp.float32)
+    first = lax.broadcasted_iota(jnp.int32, (pad, slots), 0) == 0
+    table = items_ref[k].reshape(n_col * depth, rank).T
+    left = jnp.concatenate([table[:, h * TILE : (h + 1) * TILE] for h in range(halves)], axis=0)
+    packed = slot_ref[k].astype(jnp.float32)
+    low, high, rate = packed[:, :slots], packed[:, slots : 2 * slots], packed[:, 2 * slots :]
+    here = pl.ds(pl.multiple_of(k * slots, slots), slots)
+    for u in range(users):
+        hot = (entry == low[u : u + 1]).astype(jnp.bfloat16)
+        picked = jnp.dot(left, hot, preferred_element_type=jnp.float32)
+        rows = jnp.zeros((rank, slots), jnp.float32)
+        for h in range(halves):
+            rows = jnp.where(high[u : u + 1] == h, picked[h * rank : (h + 1) * rank], rows)
+        x_ref[u, 0:rank, here] = rows.astype(jnp.bfloat16)
+        x_ref[u, rank:, here] = jnp.where(first, rate[u : u + 1], 0.0).astype(jnp.bfloat16)
+    return number + jnp.sum((high >= 0).astype(jnp.float32), axis=1, keepdims=True)
+
+
+def gather_kernel(
+    n_row, n_col, item_ref, slot_ref, full_ref, number_ref,
+    all_ref, got_ref, x_ref, own_sem, z_sem, far_sem, near_sem, slot_sem,
+):
     row, col = lax.axis_index("row"), lax.axis_index("col")
     half = n_row // 2
     twin = row + 1 - 2 * lax.rem(row, 2)
@@ -204,37 +203,85 @@
     for d in range(1, n_col):
         along[d].wait_recv()
         spread(d, all_ref.at[row, lax.rem(col - d + n_col, n_col)])
-    for d in range(n_col):
+    own_items.wait()
+    own_slots.wait()
+    for copy in slots:
+        copy.wait_recv()
+    users, rank = number_ref.shape
+    number = place_block(all_ref, got_ref, x_ref, row, jnp.zeros((users, 1), jnp.float32))
+
+    def across_copy(d, e):
         piece = lax.rem(col - d + n_col, n_col)
-        for e in range(1, half):
-            across[d, e].wait_recv()
-            source = lax.rem(row - 2 * e + n_row, n_row)
-            sems = near_sem.at[0, d, e], near_sem.at[1, d, e]
-            pair[d, e] = send(all_ref.at[source, piece], all_ref.at[source, piece], sems, (twin, col))
+        source = lax.rem(row - 2 * e + n_row, n_row)
+        return pltpu.make_async_remote_copy(
+            src_ref=all_ref.at[source, piece],
+            dst_ref=all_ref.at[source, piece],
+            send_sem=far_sem.at[0, d, e],
+            recv_sem=far_sem.at[1, d, e],
+            device_id=(far(e), col),
+            device_id_type=pl.DeviceIdType.MESH,
+        )
+
+    def pair_copy(d, e, start):
+        piece = lax.rem(col - d + n_col, n_col)
+        source = lax.rem(start - 2 * e + n_row, n_row)
+        return pltpu.make_async_remote_copy(
+            src_ref=all_ref.at[source, piece],
+            dst_ref=all_ref.at[source, piece],
+            send_sem=near_sem.at[0, d, e],
+            recv_sem=near_sem.at[1, d, e],
+            device_id=(twin, col),
+            device_id_type=pl.DeviceIdType.MESH,
+        )
+
+    def same_core(e, number):
+        for d in range(n_col):
+            across_copy(d, e).wait_recv()
+            pair_copy(d, e, row).start()
+        return place_block(all_ref, got_ref, x_ref, lax.rem(row - 2 * e + n_row, n_row), number)
+
+    number = lax.fori_loop(1, half, same_core, number)
+
+    def other_core(e, number):
+        for d in range(n_col):
+            pair_copy(d, e, twin).wait_recv()
+        return place_block(all_ref, got_ref, x_ref, lax.rem(twin - 2 * e + n_row, n_row), number)
+
+    number = lax.fori_loop(0, half, other_core, number)
+    number_ref[...] = jnp.broadcast_to(number, (users, rank))
+
+    for u in range(users):
+        full_ref[u] = lax.dot_general(
+            x_ref[u], x_ref[u, 0:rank, :], (((1,), (1,)), ((), ())), preferred_element_type=jnp.float32
+        )
+
     for copy in slots:
-        copy.wait()
+        copy.wait_send()
     for copy in along.values():
         copy.wait_send()
     for copy in across.values():
         copy.wait_send()
-    for copy in pair.values():
-        copy.wait()
-    own_items.wait()
-    own_slots.wait()
-
-
-def exchange(n_row, n_col, items, packed):
+    for d in range(n_col):
+        for e in range(half):
+            pair_copy(d, e, row).wait_send()
+
+
+def gather(n_row, n_col, items, packed):
     half = n_row // 2
+    users, slots, rank = packed.shape[1], packed.shape[2] // 3, items.shape[1]
     vmem = pl.BlockSpec(memory_space=pltpu.VMEM)
     return pl.pallas_call(
-        functools.partial(exchange_kernel, n_row, n_col),
+        functools.partial(gather_kernel, n_row, n_col),
         out_shape=(
-            jax.ShapeDtypeStruct((n_row, n_col) + items.shape, items.dtype),
-            jax.ShapeDtypeStruct(packed.shape, packed.dtype),
+            jax.ShapeDtypeStruct((users, rank + 16, rank), jnp.float32),
+            jax.ShapeDtypeStruct((users, rank), jnp.float32),
         ),
         in_specs=[vmem] * 2,
         out_specs=(vmem, vmem),
         scratch_shapes=[
+            pltpu.VMEM((n_row, n_col) + items.shape, items.dtype),
+            pltpu.VMEM(packed.shape, packed.dtype),
+            pltpu.VMEM((users, rank + 16, n_row * slots), jnp.bfloat16),
             pltpu.SemaphoreType.DMA((2,)),
             pltpu.SemaphoreType.DMA((2, n_col)),
             pltpu.SemaphoreType.DMA((2, n_col, half)),
@@ -242,20 +289,18 @@
             pltpu.SemaphoreType.DMA((2, n_row)),
         ],
         compiler_params=pltpu.CompilerParams(
-            collective_id=0, has_side_effects=True, vmem_limit_bytes=24 * 1024 * 1024
+            collective_id=0, has_side_effects=True, vmem_limit_bytes=48 * 1024 * 1024
         ),
     )(items, packed)
 
 
 def per_device(n_row, n_col, item_factors, item_index, ratings, counts):
-    rank = item_factors.shape[1]
     users, slots = item_index.shape
     live = lax.broadcasted_iota(jnp.int32, item_index.shape, 1) < counts
     low = (item_index % TILE).astype(jnp.bfloat16)
     high = jnp.where(live, item_index // TILE, -1).astype(jnp.bfloat16)
     packed = jnp.concatenate([low, high, ratings], axis=1).reshape(n_row, users // n_row, 3 * slots)
-    items, moved = exchange(n_row, n_col, item_factors, packed)
-    return solve(items.reshape(n_row, -1, rank), moved, rank)[None]
+    return solve(*gather(n_row, n_col, item_factors, packed))[None]
 
 
 def solution(mesh):

time: 35.7 us -> 33.3 us (0.933)
  Pallas kernels: 33.1 us -> 30.7 us
    pallas_call x2, Pallas kernels: 33.1 us -> 30.7 us  [the longest x1 19.9 us: gather(): pl.pallas_call(functools.partial(gather_kernel, n_row, n_col), out_shape=...]
where the time goes in v3:
time: 33.3 us; the launch traced here: 33.1 us
  Pallas kernels  30.7 us (92%)
  local copies, waits for them, and re-layouts  1.39 us (4%)
  other arithmetic  0.93 us (3%)
    pallas_call x1, Pallas kernels, gather(): pl.pallas_call(functools.partial(gather_kernel, n_row, n_col), out_shape=...  19.9 us
    pallas_call x1, Pallas kernels, solve(): pl.pallas_call(solve_kernel, out_shape=jax.ShapeDtypeStruct((users, rank)...  10.8 us
    unnamed x6, local copies, waits for them, and re-layouts  1.39 us
    convert_element_type x1, other arithmetic, per_device(): low = (item_index % TILE).astype(jnp.bfloat16)  0.93 us

profile of v3, /device:TPU:0, one launch (start us, length us, event | category | flops | bytes accessed | tf_op | source)
XLA Modules:
  0.0 33.1 jit_solution(440873305180377350)
XLA Ops:
  0.0 0.0 copy-start.2
  0.0 0.7 %copy-done.2 = s32[64,1]{0,1:T(1,128)S(1)} copy-done((s32[64,1]{0,1:T(1,128)S(1)}, s32[64,1]{0,1:T(1,128)}, u32[]{:S(2)}) %copy-start.2) | copy-done | bytes 280
  0.7 0.0 copy-start.1
  0.7 0.9 %fusion = (bf16[64,256]{1,0:T(8,128)(2,1)S(1)}, bf16[64,256]{1,0:T(8,128)(2,1)S(1)}) fusion(s32[64,256]{1,0:T(8,128)} %param.5, s32[64]{0:T(128)S(1)} %bitcast.4), kind=kLoop, calls=%fused_computation.6 | loop fusion | flops 376832 | bytes 131328 | tf_op jit(solution)/shard_map/convert_element_type | solution.py:300
  1.6 0.0 copy-done.1
  1.6 0.0 copy-start
  1.6 0.7 %copy-done = bf16[128,128]{1,0:T(8,128)(2,1)S(1)} copy-done((bf16[128,128]{1,0:T(8,128)(2,1)S(1)}, bf16[128,128]{1,0:T(8,128)(2,1)}, u32[]{:S(2)}) %copy-start) | copy-done | bytes 32792
  2.4 19.9 %shard_map.46 = (f32[8,144,128]{2,1,0:T(8,128)S(1)}, f32[8,128]{1,0:T(8,128)S(1)}) custom-call(bf16[128,128]{1,0:T(8,128)(2,1)S(1)} %copy-done, bf16[8,8,768]{2,1,0:T(8,128)(2,1)S(1)} %maximum_bitcast_fusion.slot_ref), custom_call_target="tpu_custom_call" | custom-call | tf_op jit(solution)/shard_map/pallas_call | solution.py:273
  22.3 10.8 %shard_map.47 = f32[8,128]{1,0:T(8,128)} custom-call(f32[8,144,128]{2,1,0:T(8,128)S(1)} %get-tuple-element.7.full_ref, f32[8,128]{1,0:T(8,128)S(1)} %get-tuple-element.8.number_ref), custom_call_target="tpu_custom_call" | custom-call | tf_op jit(solution)/shard_map/pallas_call | solution.py:106
  (1 shorter events, 0.0 us)
Async XLA Ops:
  0.0 0.7 %copy-start.2 = (s32[64,1]{0,1:T(1,128)S(1)}, s32[64,1]{0,1:T(1,128)}, u32[]{:S(2)}) copy-start(s32[64,1]{0,1:T(1,128)} %param.7) | copy-start | bytes 772
  0.7 0.9 %copy-start.1 = (bf16[64,256]{1,0:T(8,128)(2,1)S(1)}, bf16[64,256]{1,0:T(8,128)(2,1)}, u32[]{:S(2)}) copy-start(bf16[64,256]{1,0:T(8,128)(2,1)} %param.6) | copy-start | bytes 98308
  1.6 0.8 %copy-start = (bf16[128,128]{1,0:T(8,128)(2,1)S(1)}, bf16[128,128]{1,0:T(8,128)(2,1)}, u32[]{:S(2)}) copy-start(bf16[128,128]{1,0:T(8,128)(2,1)} %item_ref.1) | copy-start | bytes 98308

commit v4 on v3

--- a/solution.py
+++ b/solution.py
@@ -15,6 +15,13 @@
 def lane(x, i):
     where = jnp.full(x.shape, i, jnp.int32)
     return jnp.take_along_axis(x, where, axis=1, mode="promise_in_bounds")
+
+
+def split(x):
+    x0 = x.astype(jnp.bfloat16)
+    rest = x - x0.astype(jnp.float32)
+    x1 = rest.astype(jnp.bfloat16)
+    return x0, x1, (rest - x1.astype(jnp.float32)).astype(jnp.bfloat16)
 
 
 def factor_and_solve(a_ref, l_ref, s_ref, y, shift, users, rank):
@@ -72,10 +79,11 @@
         if done < rank:
             for u in range(users):
                 mine = pl.ds(u, GROUP, stride=users)
-                left = s_ref[0, mine, :].T[done:]
-                update = jnp.dot(
-                    left, s_ref[1, mine, :], precision=lax.Precision.HIGHEST, preferred_element_type=jnp.float32
-                )
+                l0, l1, l2 = split(s_ref[0, mine, :])
+                r0, r1, r2 = split(s_ref[1, mine, :])
+                left = jnp.concatenate([l0, l0, l1, l0, l2, l1], axis=0)
+                right = jnp.concatenate([r0, r1, r0, r2, r0, r1], axis=0)
+                update = jnp.dot(left.T[done:], right, preferred_element_type=jnp.float32)
                 rest = pl.ds(done * users + u, rank - done, stride=users)
                 a_ref[rest, :] = a_ref[rest, :] - update
     y, inv_diag = carry
@@ -141,8 +149,8 @@
 
 
 def gather_kernel(
-    n_row, n_col, item_ref, slot_ref, full_ref, number_ref,
-    all_ref, got_ref, x_ref, own_sem, z_sem, far_sem, near_sem, slot_sem,
+    n_row, n_col, item_ref, index_ref, rate_ref, count_ref, full_ref, number_ref,
+    slot_ref, all_ref, got_ref, x_ref, own_sem, z_sem, far_sem, near_sem, slot_sem,
 ):
     row, col = lax.axis_index("row"), lax.axis_index("col")
     half = n_row // 2
@@ -162,6 +170,17 @@
         pl.semaphore_signal(barrier, inc=1, device_id=(row, col_at(d)), device_id_type=pl.DeviceIdType.MESH)
     for d in range(1, n_row):
         pl.semaphore_signal(barrier, inc=1, device_id=(row_at(d), col), device_id_type=pl.DeviceIdType.MESH)
+
+    users, rank = number_ref.shape
+    slots_each = index_ref.shape[1]
+    live = lax.broadcasted_iota(jnp.int32, index_ref.shape, 1) < count_ref[...]
+    low = lax.rem(index_ref[...], TILE).astype(jnp.float32)
+    high = jnp.where(live, lax.div(index_ref[...], TILE), -1).astype(jnp.float32)
+    rate = rate_ref[...].astype(jnp.float32)
+    for r in range(n_row):
+        for part, values in enumerate((low, high, rate)):
+            mine = values[r * users : (r + 1) * users].astype(jnp.bfloat16)
+            slot_ref[r, :, part * slots_each : (part + 1) * slots_each] = mine
 
     own_items = pltpu.make_async_copy(item_ref, all_ref.at[row, col], own_sem.at[0])
     own_items.start()
@@ -207,9 +226,6 @@
     own_slots.wait()
     for copy in slots:
         copy.wait_recv()
-    users, rank = number_ref.shape
-    number = place_block(all_ref, got_ref, x_ref, row, jnp.zeros((users, 1), jnp.float32))
-
     def across_copy(d, e):
         piece = lax.rem(col - d + n_col, n_col)
         source = lax.rem(row - 2 * e + n_row, n_row)
@@ -234,20 +250,33 @@
             device_id_type=pl.DeviceIdType.MESH,
         )
 
-    def same_core(e, number):
-        for d in range(n_col):
+    def forward(d):
+        for e in range(1, half):
             across_copy(d, e).wait_recv()
             pair_copy(d, e, row).start()
-        return place_block(all_ref, got_ref, x_ref, lax.rem(row - 2 * e + n_row, n_row), number)
-
-    number = lax.fori_loop(1, half, same_core, number)
-
-    def other_core(e, number):
+
+    def place(start, e, number):
+        return place_block(all_ref, got_ref, x_ref, lax.rem(start - 2 * e + n_row, n_row), number)
+
+    def arrive(e):
         for d in range(n_col):
             pair_copy(d, e, twin).wait_recv()
-        return place_block(all_ref, got_ref, x_ref, lax.rem(twin - 2 * e + n_row, n_row), number)
-
-    number = lax.fori_loop(0, half, other_core, number)
+
+    forward(0)
+    number = place(row, 0, jnp.zeros((users, 1), jnp.float32))
+    for d in range(1, n_col // 2):
+        forward(d)
+    arrive(0)
+    number = place(twin, 0, number)
+    for d in range(max(1, n_col // 2), n_col):
+        forward(d)
+    number = lax.fori_loop(1, half, functools.partial(place, row), number)
+
+    def other_core(e, number):
+        arrive(e)
+        return place(twin, e, number)
+
+    number = lax.fori_loop(1, half, other_core, number)
     number_ref[...] = jnp.broadcast_to(number, (users, rank))
 
     for u in range(users):
@@ -266,9 +295,10 @@
             pair_copy(d, e, row).wait_send()
 
 
-def gather(n_row, n_col, items, packed):
+def gather(n_row, n_col, items, index, ratings, counts):
     half = n_row // 2
-    users, slots, rank = packed.shape[1], packed.shape[2] // 3, items.shape[1]
+    users, slots, rank = index.shape[0] // n_row, index.shape[1], items.shape[1]
+    packed = pltpu.VMEM((n_row, users, 3 * slots), jnp.bfloat16)
     vmem = pl.BlockSpec(memory_space=pltpu.VMEM)
     return pl.pallas_call(
         functools.partial(gather_kernel, n_row, n_col),
@@ -276,11 +306,12 @@
             jax.ShapeDtypeStruct((users, rank + 16, rank), jnp.float32),
             jax.ShapeDtypeStruct((users, rank), jnp.float32),
         ),
-        in_specs=[vmem] * 2,
+        in_specs=[vmem] * 4,
         out_specs=(vmem, vmem),
         scratch_shapes=[
+            packed,
             pltpu.VMEM((n_row, n_col) + items.shape, items.dtype),
-            pltpu.VMEM(packed.shape, packed.dtype),
+            packed,
             pltpu.VMEM((users, rank + 16, n_row * slots), jnp.bfloat16),
             pltpu.SemaphoreType.DMA((2,)),
             pltpu.SemaphoreType.DMA((2, n_col)),
@@ -291,16 +322,11 @@
         compiler_params=pltpu.CompilerParams(
             collective_id=0, has_side_effects=True, vmem_limit_bytes=48 * 1024 * 1024
         ),
-    )(items, packed)
+    )(items, index, ratings, counts)
 
 
 def per_device(n_row, n_col, item_factors, item_index, ratings, counts):
-    users, slots = item_index.shape
-    live = lax.broadcasted_iota(jnp.int32, item_index.shape, 1) < counts
-    low = (item_index % TILE).astype(jnp.bfloat16)
-    high = jnp.where(live, item_index // TILE, -1).astype(jnp.bfloat16)
-    packed = jnp.concatenate([low, high, ratings], axis=1).reshape(n_row, users // n_row, 3 * slots)
-    return solve(*gather(n_row, n_col, item_factors, packed))[None]
+    return solve(*gather(n_row, n_col, item_factors, item_index, ratings, counts))[None]
 
 
 def solution(mesh):

time: 33.3 us -> 31.7 us (0.952)
  Pallas kernels: 30.7 us -> 29 us
  local copies, waits for them, and re-layouts: 1.39 us -> 2.37 us
  other arithmetic: 0.93 us -> 0 us
    pallas_call x1, Pallas kernels: 10.8 us -> 9.44 us  [solve(): pl.pallas_call(solve_kernel, out_shape=jax.ShapeDtypeStruct((users, rank)...]
    unnamed x6 -> x7, local copies, waits for them, and re-layouts: 1.39 us -> 2.37 us
    convert_element_type x1 -> x0, other arithmetic: 0.93 us -> none  [per_device(): low = (item_index % TILE).astype(jnp.bfloat16)]
    pallas_call x1, Pallas kernels: 19.9 us -> 19.6 us  [gather(): pl.pallas_call(functools.partial(gather_kernel, n_row, n_col), out_shape=...]
where the time goes in v4:
time: 31.7 us; the launch traced here: 31.4 us
  Pallas kernels  29 us (91%)
  local copies, waits for them, and re-layouts  2.37 us (7%)
    pallas_call x1, Pallas kernels, gather(): pl.pallas_call(functools.partial(gather_kernel, n_row, n_col), out_shape=...  19.6 us
    pallas_call x1, Pallas kernels, solve(): pl.pallas_call(solve_kernel, out_shape=jax.ShapeDtypeStruct((users, rank)...  9.44 us
    unnamed x7, local copies, waits for them, and re-layouts  2.37 us

profile of v4, /device:TPU:0, one launch (start us, length us, event | category | flops | bytes accessed | tf_op | source)
XLA Modules:
  0.0 31.4 jit_solution(1586634258352907928)
XLA Ops:
  0.0 0.0 copy-start.1
  0.0 0.8 %copy.5.count_ref = s32[64,1]{1,0:T(8,128)S(1)} copy(s32[64,1]{0,1:T(1,128)} %param.7) | data formatting | bytes 512 | tf_op args[3]
  0.8 0.0 copy-done.1
  0.8 0.0 copy-start
  0.8 0.8 %copy-done = s32[64,256]{1,0:T(8,128)S(1)} copy-done((s32[64,256]{1,0:T(8,128)S(1)}, s32[64,256]{1,0:T(8,128)}, u32[]{:S(2)}) %copy-start) | copy-done | bytes 65560
  1.6 0.0 copy-start.2
  1.6 0.8 %copy-done.2 = bf16[64,256]{1,0:T(8,128)(2,1)S(1)} copy-done((bf16[64,256]{1,0:T(8,128)(2,1)S(1)}, bf16[64,256]{1,0:T(8,128)(2,1)}, u32[]{:S(2)}) %copy-start.2) | copy-done | bytes 32792
  2.4 19.6 %shard_map.46 = (f32[8,144,128]{2,1,0:T(8,128)S(1)}, f32[8,128]{1,0:T(8,128)S(1)}) custom-call(bf16[128,128]{1,0:T(8,128)(2,1)S(1)} %copy-done.1, s32[64,256]{1,0:T(8,128)S(1)} %copy-done, bf16[64,256]{1,0:T(8,128)(2,1)S(1)} %copy-done.2, s32[64,1]{1,0:T(8,128)S(1)} %copy.5.count_ref), custom_call_target="tpu_custom_call" | custom-call | tf_op jit(solution)/shard_map/pallas_call | solution.py:303
  22.0 9.4 %shard_map.47 = f32[8,128]{1,0:T(8,128)} custom-call(f32[8,144,128]{2,1,0:T(8,128)S(1)} %get-tuple-element.7.full_ref, f32[8,128]{1,0:T(8,128)S(1)} %get-tuple-element.8.number_ref), custom_call_target="tpu_custom_call" | custom-call | tf_op jit(solution)/shard_map/pallas_call | solution.py:114
Async XLA Ops:
  0.0 0.8 %copy-start.1 = (bf16[128,128]{1,0:T(8,128)(2,1)S(1)}, bf16[128,128]{1,0:T(8,128)(2,1)}, u32[]{:S(2)}) copy-start(bf16[128,128]{1,0:T(8,128)(2,1)} %item_ref.1) | copy-start | bytes 98308
  0.8 0.8 %copy-start = (s32[64,256]{1,0:T(8,128)S(1)}, s32[64,256]{1,0:T(8,128)}, u32[]{:S(2)}) copy-start(s32[64,256]{1,0:T(8,128)} %index_ref.1) | copy-start | bytes 196612
  1.6 0.8 %copy-start.2 = (bf16[64,256]{1,0:T(8,128)(2,1)S(1)}, bf16[64,256]{1,0:T(8,128)(2,1)}, u32[]{:S(2)}) copy-start(bf16[64,256]{1,0:T(8,128)(2,1)} %rate_ref.1) | copy-start | bytes 98308

commit v5 on v4

--- a/solution.py
+++ b/solution.py
@@ -149,8 +149,8 @@
 
 
 def gather_kernel(
-    n_row, n_col, item_ref, index_ref, rate_ref, count_ref, full_ref, number_ref,
-    slot_ref, all_ref, got_ref, x_ref, own_sem, z_sem, far_sem, near_sem, slot_sem,
+    n_row, n_col, item_ref, index_in, rate_in, count_in, full_ref, number_ref,
+    index_ref, rate_ref, count_ref, in_sem, slot_ref, all_ref, got_ref, x_ref, own_sem, z_sem, far_sem, near_sem, slot_sem,
 ):
     row, col = lax.axis_index("row"), lax.axis_index("col")
     half = n_row // 2
@@ -171,21 +171,12 @@
     for d in range(1, n_row):
         pl.semaphore_signal(barrier, inc=1, device_id=(row_at(d), col), device_id_type=pl.DeviceIdType.MESH)
 
-    users, rank = number_ref.shape
-    slots_each = index_ref.shape[1]
-    live = lax.broadcasted_iota(jnp.int32, index_ref.shape, 1) < count_ref[...]
-    low = lax.rem(index_ref[...], TILE).astype(jnp.float32)
-    high = jnp.where(live, lax.div(index_ref[...], TILE), -1).astype(jnp.float32)
-    rate = rate_ref[...].astype(jnp.float32)
-    for r in range(n_row):
-        for part, values in enumerate((low, high, rate)):
-            mine = values[r * users : (r + 1) * users].astype(jnp.bfloat16)
-            slot_ref[r, :, part * slots_each : (part + 1) * slots_each] = mine
-
+    loads = []
+    for n, (src, dst) in enumerate(((index_in, index_ref), (rate_in, rate_ref), (count_in, count_ref))):
+        loads.append(pltpu.make_async_copy(src, dst, in_sem.at[n]))
+        loads[-1].start()
     own_items = pltpu.make_async_copy(item_ref, all_ref.at[row, col], own_sem.at[0])
     own_items.start()
-    own_slots = pltpu.make_async_copy(slot_ref.at[row], got_ref.at[row], own_sem.at[1])
-    own_slots.start()
     pl.semaphore_wait(barrier, n_col + n_row - 2)
 
     def send(src, dst, sems, where):
@@ -215,6 +206,24 @@
         pair[d, 0] = send(src, all_ref.at[row, piece], sems, (twin, col))
 
     spread(0, item_ref)
+    for copy in loads:
+        copy.wait()
+    users, rank = number_ref.shape
+    slots_each = index_ref.shape[1]
+    square = (index_ref.shape[0],) * 2
+    same = lax.broadcasted_iota(jnp.int32, square, 0) == lax.broadcasted_iota(jnp.int32, square, 1)
+    count = jnp.sum(jnp.where(same, count_ref[...].astype(jnp.float32), 0.0), axis=1, keepdims=True)
+    live = lax.broadcasted_iota(jnp.int32, index_ref.shape, 1).astype(jnp.float32) < count
+    low = lax.rem(index_ref[...], TILE).astype(jnp.float32)
+    high = jnp.where(live, lax.div(index_ref[...], TILE), -1).astype(jnp.float32)
+    rate = rate_ref[...].astype(jnp.float32)
+    for r in range(n_row):
+        for part, values in enumerate((low, high, rate)):
+            mine = values[r * users : (r + 1) * users].astype(jnp.bfloat16)
+            slot_ref[r, :, part * slots_each : (part + 1) * slots_each] = mine
+
+    own_slots = pltpu.make_async_copy(slot_ref.at[row], got_ref.at[row], own_sem.at[1])
+    own_slots.start()
     slots = []
     for d in range(1, n_row):
         to = row_at(d)
@@ -306,9 +315,13 @@
             jax.ShapeDtypeStruct((users, rank + 16, rank), jnp.float32),
             jax.ShapeDtypeStruct((users, rank), jnp.float32),
         ),
-        in_specs=[vmem] * 4,
+        in_specs=[pl.BlockSpec(memory_space=pltpu.HBM)] * 4,
         out_specs=(vmem, vmem),
         scratch_shapes=[
+            pltpu.VMEM(index.shape, index.dtype),
+            pltpu.VMEM(ratings.shape, ratings.dtype),
+            pltpu.VMEM((1, counts.shape[0]), counts.dtype),
+            pltpu.SemaphoreType.DMA((3,)),
             packed,
             pltpu.VMEM((n_row, n_col) + items.shape, items.dtype),
             packed,
@@ -320,9 +333,9 @@
             pltpu.SemaphoreType.DMA((2, n_row)),
         ],
         compiler_params=pltpu.CompilerParams(
-            collective_id=0, has_side_effects=True, vmem_limit_bytes=48 * 1024 * 1024
+            collective_id=0, has_side_effects=True, vmem_limit_bytes=60 * 1024 * 1024
         ),
-    )(items, index, ratings, counts)
+    )(items, index, ratings, counts.reshape(1, -1))
 
 
 def per_device(n_row, n_col, item_factors, item_index, ratings, counts):

time: 31.7 us -> 32 us (level)
  Pallas kernels: 29 us -> 30 us
  local copies, waits for them, and re-layouts: 2.37 us -> 1.73 us
    pallas_call x1, Pallas kernels: 19.6 us -> 20.6 us  [gather(): pl.pallas_call(functools.partial(gather_kernel, n_row, n_col), out_shape=...]
    unnamed x7 -> x4, local copies, waits for them, and re-layouts: 2.37 us -> 1.73 us
where the time goes in v5:
time: 32 us; the launch traced here: 31.8 us
  Pallas kernels  30 us (94%)
  local copies, waits for them, and re-layouts  1.73 us (5%)
    pallas_call x1, Pallas kernels, gather(): pl.pallas_call(functools.partial(gather_kernel, n_row, n_col), out_shape=...  20.6 us
    pallas_call x1, Pallas kernels, solve(): pl.pallas_call(solve_kernel, out_shape=jax.ShapeDtypeStruct((users, rank)...  9.43 us
    unnamed x4, local copies, waits for them, and re-layouts  1.73 us

profile of v5, /device:TPU:0, one launch (start us, length us, event | category | flops | bytes accessed | tf_op | source)
XLA Modules:
  0.0 31.8 jit_solution(15136826063836443260)
XLA Ops:
  0.0 20.6 %shard_map.46 = (f32[8,144,128]{2,1,0:T(8,128)}, f32[8,128]{1,0:T(8,128)}) custom-call(bf16[128,128]{1,0:T(8,128)(2,1)} %item_ref.1, s32[64,256]{1,0:T(8,128)} %index_in.1, bf16[64,256]{1,0:T(8,128)(2,1)} %rate_in.1, s32[1,64]{1,0:T(1,128)} %bitcast.2), custom_call_target="tpu_custom_call" | custom-call | tf_op jit(solution)/shard_map/pallas_call | solution.py:312
  20.6 0.0 copy-start
  20.6 1.1 %copy-done = f32[8,144,128]{2,1,0:T(8,128)S(1)} copy-done((f32[8,144,128]{2,1,0:T(8,128)S(1)}, f32[8,144,128]{2,1,0:T(8,128)}, u32[]{:S(2)}) %copy-start) | copy-done | bytes 589848
  21.7 0.0 copy-start.1
  21.7 0.7 %copy-done.1 = f32[8,128]{1,0:T(8,128)S(1)} copy-done((f32[8,128]{1,0:T(8,128)S(1)}, f32[8,128]{1,0:T(8,128)}, u32[]{:S(2)}) %copy-start.1) | copy-done | bytes 4120
  22.4 9.4 %shard_map.47 = f32[8,128]{1,0:T(8,128)} custom-call(f32[8,144,128]{2,1,0:T(8,128)S(1)} %copy-done, f32[8,128]{1,0:T(8,128)S(1)} %copy-done.1), custom_call_target="tpu_custom_call" | custom-call | tf_op jit(solution)/shard_map/pallas_call | solution.py:114
Async XLA Ops:
  20.6 1.1 %copy-start = (f32[8,144,128]{2,1,0:T(8,128)S(1)}, f32[8,144,128]{2,1,0:T(8,128)}, u32[]{:S(2)}) copy-start(f32[8,144,128]{2,1,0:T(8,128)} %get-tuple-element.7.full_ref) | copy-start | bytes 1769476
  21.7 0.7 %copy-start.1 = (f32[8,128]{1,0:T(8,128)S(1)}, f32[8,128]{1,0:T(8,128)}, u32[]{:S(2)}) copy-start(f32[8,128]{1,0:T(8,128)} %get-tuple-element.8.number_ref) | copy-start | bytes 12292
